TPU v7x, 32 devices: a whole 2x2x4 slice. The times are simulated.
32 devices in a mesh: groups: 2 (over y), seg: 4 (over z), ctx: 2 (over x), head: 2 (over core).
Axes of the slice: x: 2, y: 2, z: 4, core: 2. Of those that a mesh axis runs over, the one named last changes fastest.
Arguments:
- queries: bfloat16 [1024, 1024], P(('groups', 'ctx'), 'head'), parts along dimension 0, may hold values from -40 to 40
- cached_keys: bfloat16 [4096, 128], P(('groups', 'seg', 'ctx')), parts along dimension 0, may hold values from -20 to 20
- cached_values: bfloat16 [4096, 128], P(('groups', 'seg', 'ctx')), parts along dimension 0, may hold values from -6 to 6
- key_offsets: int32 [16], P('groups'), parts along dimension 0, may hold values from 0 to 1792, as said below
- vertical_blocks: int32 [16, 16], P('groups'), parts along dimension 0, may hold values from 0 to 31
- slash_offsets: int32 [16, 32], P('groups'), parts along dimension 0, may hold values from 0 to 24, as said below
Outputs:
- attended: bfloat16 [1024, 1024], P(('groups', 'ctx'), 'head'), parts along dimension 0
There are 2 independent parts, one for each index of `groups`. A program takes and returns all parts, laid end to end along the dimension named above; each array names one. Nothing has to cross between parts.
Inputs may be any that keep to these rules, and one draw needn't show every extreme that they name: `key_offsets`: holds k * 256 for every k below the number of key shards, each once. `slash_offsets`: column 0 is 0 in every row.
All inputs are finite; a program needn't handle non-finite values.
Results may differ from a plain program's by a relative error of at most 0.028.
Values may be sent and summed in bfloat16 or wider, within the bound.
A program may use at most 64 MiB of HBM per device.

v0:
```python
import math

import jax
import jax.numpy as jnp
from jax import lax
from jax.sharding import PartitionSpec as P

HEAD_DIM = 128
BLOCK = 64


ROPE_THETA = 500000.0
ROPE_FACTOR = 8.0
LOW_FACTOR = 1.0
HIGH_FACTOR = 4.0
TRAINED_CONTEXT = 8192.0
MASKED_SCORE = -1e30


def combined_all(shard, axis, join):
    gathered = jax.tree.map(
        lambda a, kind: lax.all_gather(a.astype(kind), axis),
        shard,
        (jnp.bfloat16, jnp.bfloat16, jnp.bfloat16),
    )

    def take(source):
        return jax.tree.map(
            lambda a, own: lax.dynamic_index_in_dim(a, source, 0, False).astype(own.dtype),
            gathered,
            shard,
        )

    return lax.fori_loop(
        1, lax.axis_size(axis), lambda source, state: join(state, take(source)), take(0)
    )


def inverse_frequencies(vector_width):
    exponent = jnp.arange(0, vector_width, 2, dtype=jnp.float32) / vector_width
    base_frequency = 1.0 / ROPE_THETA**exponent
    wavelength = 2.0 * math.pi / base_frequency
    smooth = (TRAINED_CONTEXT / wavelength - LOW_FACTOR) / (HIGH_FACTOR - LOW_FACTOR)
    blended = (1.0 - smooth) * base_frequency / ROPE_FACTOR + smooth * base_frequency
    return jnp.where(
        wavelength < TRAINED_CONTEXT / HIGH_FACTOR,
        base_frequency,
        jnp.where(wavelength > TRAINED_CONTEXT / LOW_FACTOR, base_frequency / ROPE_FACTOR, blended),
    )


def rotate(vectors, positions):
    vector_width = vectors.shape[-1]
    half_width = vector_width // 2
    angles = positions.astype(jnp.float32)[:, None] * inverse_frequencies(vector_width)[None, :]
    cosine = jnp.concatenate([jnp.cos(angles), jnp.cos(angles)], axis=-1)[:, None, :]
    sine_table = jnp.concatenate([jnp.sin(angles), jnp.sin(angles)], axis=-1)[:, None, :]
    widened = vectors.astype(jnp.float32)
    turned = jnp.concatenate([-widened[..., half_width:], widened[..., :half_width]], axis=-1)
    return (widened * cosine + turned * sine_table).astype(jnp.bfloat16)


def combine_partials(earlier, later):
    joined_max = jnp.maximum(earlier[0], later[0])
    earlier_scale = jnp.exp(earlier[0] - joined_max)
    later_scale = jnp.exp(later[0] - joined_max)
    numerator = earlier[1] * earlier_scale[:, None] + later[1] * later_scale[:, None]
    denominator = earlier[2] * earlier_scale + later[2] * later_scale
    return (joined_max, numerator, denominator)


def local(queries, cached_keys, cached_values, key_offsets, vertical_blocks, slash_offsets):
    query_rows = queries.shape[0]
    heads_here = queries.shape[1] // HEAD_DIM
    shard_keys = cached_keys.shape[0]
    cycle_size = lax.axis_size("ctx")
    prefix = shard_keys * lax.axis_size("seg") * cycle_size - query_rows * cycle_size
    query_start = prefix + lax.axis_index("ctx") * query_rows
    query_positions = query_start + jnp.arange(query_rows, dtype=jnp.int32)
    flat_rows = query_rows * heads_here
    rotated_queries = rotate(
        queries.reshape(query_rows, heads_here, HEAD_DIM), query_positions
    ).reshape(flat_rows, HEAD_DIM)
    segment_base = lax.axis_index("seg") * cycle_size
    segment_offsets = lax.dynamic_slice_in_dim(key_offsets, segment_base, cycle_size, 0)
    own_offset = lax.dynamic_slice_in_dim(key_offsets, segment_base + lax.axis_index("ctx"), 1, 0)[
        0
    ]
    own_positions = own_offset + jnp.arange(shard_keys, dtype=jnp.int32)
    rotated_keys = rotate(cached_keys.reshape(shard_keys, 1, HEAD_DIM), own_positions).reshape(
        shard_keys, HEAD_DIM
    )
    block_count = query_rows // BLOCK
    list_start = (query_start - prefix) // BLOCK
    vertical_rows = lax.dynamic_slice_in_dim(vertical_blocks, list_start, block_count, 0)
    slash_rows = lax.dynamic_slice_in_dim(slash_offsets, list_start, block_count, 0)
    query_blocks = query_start // BLOCK + jnp.arange(block_count, dtype=jnp.int32)
    score_scale = HEAD_DIM ** (-0.5)

    def attend_keys(carried, key_tile, value_tile, key_positions):
        key_block = key_positions // BLOCK
        vertical_hit = jnp.any(vertical_rows[:, :, None] == key_block[None, None, :], axis=1)
        distance = query_blocks[:, None] - key_block[None, :]
        slash_hit = jnp.any(slash_rows[:, :, None] == distance[:, None, :], axis=1)
        allowed = jnp.repeat(vertical_hit | slash_hit, BLOCK, axis=0) & (
            key_positions[None, :] <= query_positions[:, None]
        )
        running_max, numerator, denominator = carried
        parts_max, parts_num, parts_den = ([], [], [])
        tile_mask = jnp.repeat(allowed, heads_here, axis=0)
        query_tile = rotated_queries
        current = (running_max, numerator, denominator)

        def update(pieces, tile_mask=tile_mask, query_tile=query_tile):
            old_max, old_num, old_den = pieces
            scores = (
                jnp.einsum("qd,kd->qk", query_tile, key_tile, preferred_element_type=jnp.float32)
                * score_scale
            )
            scores = jnp.where(tile_mask, scores, MASKED_SCORE)
            fresh_max = jnp.maximum(old_max, jnp.max(scores, axis=1))
            weights = jnp.where(tile_mask, jnp.exp(scores - fresh_max[:, None]), 0.0)
            rescale = jnp.exp(old_max - fresh_max)
            product = jnp.dot(
                weights.astype(jnp.bfloat16), value_tile, preferred_element_type=jnp.float32
            )
            return (
                fresh_max,
                old_num * rescale[:, None] + product,
                old_den * rescale + jnp.sum(weights, axis=1),
            )

        def unchanged(pieces):
            return pieces

        result = lax.cond(jnp.any(tile_mask), update, unchanged, current)
        parts_max.append(result[0])
        parts_num.append(result[1])
        parts_den.append(result[2])
        return (parts_max[0], parts_num[0], parts_den[0])

    initial = (
        jnp.full((flat_rows,), MASKED_SCORE, jnp.float32),
        jnp.zeros((flat_rows, HEAD_DIM), jnp.float32),
        jnp.zeros((flat_rows,), jnp.float32),
    )
    carried = initial
    first_index = jnp.int32(0)
    key_piece = lax.all_gather(rotated_keys, "ctx", axis=0, tiled=True)
    value_piece = lax.all_gather(cached_values, "ctx", axis=0, tiled=True)
    piece_rows = key_piece.shape[0]
    key_tile = math.gcd(piece_rows, shard_keys)
    for tile_number in range(piece_rows // key_tile):
        first_key = tile_number * key_tile
        key_indices = first_index + first_key + jnp.arange(key_tile, dtype=jnp.int32)
        owner_shard = key_indices // shard_keys
        shard_match = owner_shard[:, None] == jnp.arange(cycle_size, dtype=jnp.int32)[None, :]
        offsets = jnp.sum(jnp.where(shard_match, segment_offsets[None, :], 0), axis=1)
        carried = attend_keys(
            carried,
            key_piece[first_key : first_key + key_tile],
            value_piece[first_key : first_key + key_tile],
            offsets + key_indices % shard_keys,
        )
    peak, numerator, denominator = carried
    joined = combined_all((peak, numerator, denominator), "seg", combine_partials)
    attended = (joined[1] / joined[2][:, None]).astype(jnp.bfloat16)
    return attended.reshape(query_rows, heads_here * HEAD_DIM)


def solution(mesh):
    return jax.shard_map(
        local,
        mesh=mesh,
        in_specs=(
            P(("groups", "ctx"), "head"),
            P(("groups", "seg", "ctx"), None),
            P(("groups", "seg", "ctx"), None),
            P("groups"),
            P("groups", None),
            P("groups", None),
        ),
        out_specs=P(("groups", "ctx"), "head"),
        check_vma=False,
    )
```

profile of v0, /device:TPU:1, one launch (start us, length us, event | category | flops | bytes accessed | tf_op | source)
XLA Modules:
  0.0 84.0 jit_solution(14182418264646644568)
XLA Ops:
  6.6 1.2 %reshape.318 = f32[256,4,128]{2,1,0:T(4,128)S(1)} reshape(bf16[256,512]{1,0:T(8,128)(2,1)} %param.12) | data formatting | bytes 786432 | tf_op jit(solution)/shard_map/convert_element_type | solution.py:58
  10.0 1.2 %broadcast_reduce_fusion.1 = pred[]{:T(512)} fusion(pred[256,256]{1,0:T(8,128)(4,1)S(1)} %get-tuple-element.297), kind=kLoop, calls=%fused_computation.38 | loop fusion | flops 262143 | bytes 65537 | tf_op jit(solution)/shard_map/reduce_or | solution.py:136
  11.8 1.2 %broadcast_reduce_fusion = pred[]{:T(512)} fusion(pred[256,256]{1,0:T(8,128)(4,1)S(1)} %get-tuple-element.296), kind=kLoop, calls=%fused_computation.37 | loop fusion | flops 262143 | bytes 65537 | tf_op jit(solution)/shard_map/reduce_or | solution.py:136
  14.9 1.0 %multiply_sine_fusion = (f32[256,64]{1,0:T(8,128)S(1)}, f32[256,64]{1,0:T(8,128)S(1)}, f32[256,64]{1,0:T(8,128)S(1)}, f32[256,64]{1,0:T(8,128)S(1)}) fusion(f32[256]{0:T(256)S(1)} %add_convert_fusion, f32[64]{0:T(128)S(1)} %compare_select_fusion.3, f32[256]{0:T(256)S(1)} %get-tuple-element.305), kind=kLoop, calls=%fused_computation.42 | loop fusion | flops 32768 | bytes 264448 | tf_op jit(solution)/shard_map/sin | solution.py:57
  16.5 0.7 copy-done.6
  17.5 4.3 %all_gather.24 = bf16[512,128]{1,0:T(8,128)(2,1)S(1)} all-gather(bf16[256,128]{1,0:T(8,128)(2,1)S(1)} %fusion.21), channel_id=1, replica_groups=mesh['groups'=2,'seg'=4,'ctx'=2,'head'=2] {'ctx'}, dimensions={0}, use_global_device_ids=true | all-gather | bytes 196608 | tf_op jit(solution)/shard_map/all_gather | solution.py:149
  23.6 3.8 %all_gather.25 = bf16[512,128]{1,0:T(8,128)(2,1)S(1)} all-gather(bf16[256,128]{1,0:T(8,128)(2,1)S(1)} %copy-done.7), channel_id=1, replica_groups=mesh['groups'=2,'seg'=4,'ctx'=2,'head'=2] {'ctx'}, dimensions={0}, use_global_device_ids=true | all-gather | bytes 196608 | tf_op jit(solution)/shard_map/all_gather | solution.py:150
  29.1 4.0 %conditional.2 = (f32[1024]{0:T(1024)}, f32[1024,128]{1,0:T(8,128)S(1)}, f32[1024]{0:T(1024)S(1)}) conditional(s32[]{:T(128)} %convert_element_type.122, () %tuple.41, (bf16[1024,128]{1,0:T(8,128)(2,1)S(1)}, bf16[256,128]{1,0:T(8,128)(2,1)S(1)}, pred[1024,256]{1,0:T(32,128)(4,1)S(1)}, bf16[256,128]{1,0:T(8,128)(2,1)S(1)}) %tuple.99), branch_computations={%region_8.9_spmd, %region_9.12_spmd} | conditional | flops 136712192 | bytes 5419032 | solution.py:136
  30.4 1.1 %convolution_add_fusion = f32[1024,128]{1,0:T(8,128)S(1)} fusion(bf16[256,128]{1,0:T(8,128)(2,1)S(1)} %get-tuple-element.206, pred[1024,256]{0,1:T(32,128)(4,1)S(1)} %copy.15, f32[1024,256]{0,1:T(8,128)S(1)} %get-tuple-element.283, f32[1024]{0:T(1024)} %get-tuple-element.364, f32[1024]{0:T(1024)S(1)} %get-tuple-element.270), kind=kOutput, calls=%fused_computation.2 | convolution fusion | flops 68026368 | bytes 1908736 | tf_op jit(solution)/shard_map/cond/branch_1_fun/dot_general | solution.py:124
  31.5 0.9 %fusion.1 = f32[1024]{0:T(1024)S(1)} fusion(pred[1024,256]{0,1:T(32,128)(4,1)S(1)} %copy.15, f32[1024,256]{0,1:T(8,128)S(1)} %get-tuple-element.283, f32[1024]{0:T(1024)} %get-tuple-element.364), kind=kLoop, calls=%fused_computation.4 | loop fusion | flops 785408 | bytes 1318912 | tf_op jit(solution)/shard_map/cond/branch_1_fun/reduce_sum | solution.py:130
  32.4 0.7 fusion.7
  34.1 3.7 %conditional.3 = ((f32[1024]{0:T(1024)}, f32[1024,128]{1,0:T(8,128)S(1)}, f32[1024]{0:T(1024)S(1)})) conditional(s32[]{:T(128)} %convert_element_type.121, (f32[1024]{0:T(1024)}, f32[1024,128]{1,0:T(8,128)S(1)}, f32[1024]{0:T(1024)S(1)}) %conditional.2, (pred[256,4,256]{2,1,0:T(4,128)(4,1)S(1)}, bf16[512,128]{1,0:T(8,128)(2,1)S(1)}, ...), branch_computations={%region_12.13_spmd, %region_13.16_spmd} | conditional | flops 136841216 | bytes 6488096 | solution.py:136
  35.0 0.7 max.11
  36.0 0.7 multiply_add_fusion
  37.8 0.7 convert_element_type.136
  39.2 9.8 %all-gather = bf16[4096]{0:T(1024)(128)(2,1)S(1)} all-gather(bf16[1024]{0:T(1024)(128)(2,1)S(1)} %convert_element_type.133), channel_id=2, replica_groups=mesh['groups'=2,'seg'=4,'ctx'=2,'head'=2] {'seg'}, dimensions={0}, use_global_device_ids=true | all-gather | bytes 10240 | tf_op jit(solution)/shard_map/all_gather | solution.py:22
  49.0 9.8 %all-gather.2 = bf16[4096]{0:T(1024)(128)(2,1)S(1)} all-gather(bf16[1024]{0:T(1024)(128)(2,1)S(1)} %convert_element_type.139), channel_id=4, replica_groups=mesh['groups'=2,'seg'=4,'ctx'=2,'head'=2] {'seg'}, dimensions={0}, use_global_device_ids=true | all-gather | bytes 10240 | tf_op jit(solution)/shard_map/all_gather | solution.py:22
  58.8 11.7 %all-gather.5.cloned.1.call-done = bf16[4096,128]{1,0:T(8,128)(2,1)} async-done(((bf16[1024,128]{1,0:T(8,128)(2,1)}), bf16[4096,128]{1,0:T(8,128)(2,1)}) %all-gather.5.cloned.1.call-update) | async-done | bytes 1048592 | tf_op jit(solution)/shard_map/all_gather | solution.py:22
  70.5 1.0 %slice_convert_fusion = f32[1024,128]{1,0:T(8,128)S(1)} fusion(bf16[4096,128]{1,0:T(8,128)(2,1)} %all-gather.5.cloned.1.call-done), kind=kLoop, calls=%fused_computation.39 | loop fusion | flops 131072 | bytes 786432 | tf_op jit(solution)/shard_map/convert_element_type | solution.py:29
  71.5 4.6 %while.19 = (s32[]{:T(128)}, f32[1024]{0:T(1024)S(1)}, f32[1024,128]{1,0:T(8,128)S(1)}, f32[1024]{0:T(1024)S(1)}, bf16[4,1024]{1,0:T(4,128)(2,1)S(1)}, /*index=5...) while((s32[]{:T(128)}, f32[1024]{0:T(1024)S(1)}, ...), condition=%wide.region_17.18_spmd, body=%wide.region_16.17_spmd.sunk | while | flops 532485 | bytes 1364119 | solution.py:34
  71.6 1.5 %fusion.40 = f32[1024,128]{1,0:T(8,128)S(1)} fusion(f32[1024,128]{1,0:T(8,128)S(1)} %get-tuple-element.385, f32[1024]{0:T(1024)S(1)} %get-tuple-element.358, bf16[4,1024,128]{2,1,0:T(8,128)(2,1)} %get-tuple-element.398, s32[]{:T(128)S(6)} %select_n.198, f32[1024]{0:T(1024)S(1)} %get-tuple-element.359), kind=kLoop, calls=%fused_computation.26.clone.1 | loop fusion | flops 524288 | bytes 1318916 | tf_op jit(solution)/shard_map/while/body/eval_jaxpr/add | solution.py:67
  73.1 1.5 %fusion.40 = f32[1024,128]{1,0:T(8,128)S(1)} fusion(f32[1024,128]{1,0:T(8,128)S(1)} %get-tuple-element.385, f32[1024]{0:T(1024)S(1)} %get-tuple-element.358, bf16[4,1024,128]{2,1,0:T(8,128)(2,1)} %get-tuple-element.398, s32[]{:T(128)S(6)} %select_n.198, f32[1024]{0:T(1024)S(1)} %get-tuple-element.359), kind=kLoop, calls=%fused_computation.26.clone.1 | loop fusion | flops 524288 | bytes 1318916 | tf_op jit(solution)/shard_map/while/body/eval_jaxpr/add | solution.py:67
  74.6 1.5 %fusion.40 = f32[1024,128]{1,0:T(8,128)S(1)} fusion(f32[1024,128]{1,0:T(8,128)S(1)} %get-tuple-element.385, f32[1024]{0:T(1024)S(1)} %get-tuple-element.358, bf16[4,1024,128]{2,1,0:T(8,128)(2,1)} %get-tuple-element.398, s32[]{:T(128)S(6)} %select_n.198, f32[1024]{0:T(1024)S(1)} %get-tuple-element.359), kind=kLoop, calls=%fused_computation.26.clone.1 | loop fusion | flops 524288 | bytes 1318916 | tf_op jit(solution)/shard_map/while/body/eval_jaxpr/add | solution.py:67
  76.3 0.9 %reshape.313 = bf16[256,512]{1,0:T(8,128)(2,1)} reshape(bf16[1024,128]{1,0:T(8,128)(2,1)S(1)} %divide_convert_fusion) | data formatting | bytes 524288 | tf_op jit(solution)/shard_map/reshape | solution.py:168
  (78 shorter events, 13.2 us)
Async XLA Ops:
  6.5 3.2 %copy-start = (s32[8,32]{1,0:T(8,128)S(1)}, s32[8,32]{1,0:T(8,128)}, u32[]{:S(2)}) copy-start(s32[8,32]{1,0:T(8,128)} %param.17) | copy-start | bytes 3076
  6.5 64.0 %all-gather.5.cloned.1.call-start = ((), (), s32[]{:S(2)}) async-start(), calls=%async_computation | async-start | bytes 1310720 | tf_op jit(solution)/shard_map/all_gather | solution.py:22
  6.6 1.2 %copy-start.1 = (bf16[256,512]{1,0:T(8,128)(2,1)S(1)}, bf16[256,512]{1,0:T(8,128)(2,1)}, u32[]{:S(2)}) copy-start(bf16[256,512]{1,0:T(8,128)(2,1)} %param.12) | copy-start | bytes 786436
  8.0 0.7 copy-start.9
  8.8 0.7 copy-start.8
  16.3 0.8 %copy-start.6 = (bf16[256,128]{1,0:T(8,128)(2,1)S(1)}, bf16[256,128]{1,0:T(8,128)(2,1)}, u32[]{:S(2)}) copy-start(bf16[256,128]{1,0:T(8,128)(2,1)} %param.13) | copy-start | bytes 196612
  21.8 0.7 copy-start.2
  22.7 0.8 %copy-start.7 = (bf16[256,128]{1,0:T(8,128)(2,1)S(1)}, bf16[256,128]{1,0:T(8,128)(2,1)}, u32[]{:S(2)}) copy-start(bf16[256,128]{1,0:T(8,128)(2,1)} %param.14) | copy-start | bytes 196612
  27.3 0.6 copy-start.4
  28.2 0.8 %slice-start = ((bf16[512,128]{1,0:T(8,128)(2,1)}), bf16[256,128]{1,0:T(8,128)(2,1)S(1)}, s32[]{:S(2)}) async-start(bf16[512,128]{1,0:T(8,128)(2,1)} %copy-done.2), calls=%async_computation.1 | async-start | bytes 131072 | tf_op jit(solution)/shard_map/slice | solution.py:161
  28.2 0.9 %slice-start.1 = ((bf16[512,128]{1,0:T(8,128)(2,1)}), bf16[256,128]{1,0:T(8,128)(2,1)S(1)}, s32[]{:S(2)}) async-start(bf16[512,128]{1,0:T(8,128)(2,1)} %copy-done.4), calls=%async_computation.2 | async-start | bytes 131072 | tf_op jit(solution)/shard_map/slice | solution.py:162
  33.1 0.9 %copy-start.3 = (bf16[512,128]{1,0:T(8,128)(2,1)S(1)}, bf16[512,128]{1,0:T(8,128)(2,1)}, u32[]{:S(2)}) copy-start(bf16[512,128]{1,0:T(8,128)(2,1)} %copy-done.2) | copy-start | bytes 393220
  33.1 1.0 %copy-start.5 = (bf16[512,128]{1,0:T(8,128)(2,1)S(1)}, bf16[512,128]{1,0:T(8,128)(2,1)}, u32[]{:S(2)}) copy-start(bf16[512,128]{1,0:T(8,128)(2,1)} %copy-done.4) | copy-start | bytes 393220
Sparse Core Ops, SparseCore 0:
  38.6 31.8 all-gather.4
where the time goes:
time: 85.4 us; the launch traced here: 84 us
  blocking collectives  27.7 us (32%)
  other arithmetic  16.5 us (19%)
  between operations  15 us (18%)
  waiting for transfers between devices  11.8 us (14%)
  local copies, waits for them, and re-layouts  10.6 us (12%)
  matrix products  2.3 us (3%)
    all_gather x2, blocking collectives, combined_all(): lax.all_gather(a.astype(kind), axis)  19.6 us
    all_gather x1, waiting for transfers between devices, combined_all(): lax.all_gather(a.astype(kind), axis)  11.7 us
    unnamed x20, local copies, waits for them, and re-layouts  4.68 us
    add x3, other arithmetic, combine_partials(): earlier[1] * earlier_scale[:, None] + later[1] * later_scale[:, None]  4.38 us
    all_gather x1, blocking collectives, local(): key_piece = lax.all_gather(rotated_keys, 'ctx', axis=0, tiled=True)  4.35 us
    all_gather x1, blocking collectives, local(): value_piece = lax.all_gather(cached_values, 'ctx', axis=0, tiled=True)  3.78 us
    reduce_or x2, other arithmetic, attend_keys(): result = lax.cond(jnp.any(tile_mask), update, unchanged, current)  2.35 us
  transfers between devices with their start and end apart: 1, of which 1 were waited for; matrix products, arithmetic and copies ran while one was open for 1% of the time, Pallas kernels for 0%

commit v1 on v0

v1 whole, which is shorter than its diff:
```python
import functools
import math

import jax
import jax.numpy as jnp
import numpy as np
from jax import lax
from jax.experimental import pallas as pl
from jax.experimental.pallas import tpu as pltpu
from jax.sharding import PartitionSpec as P

HEAD_DIM = 128
BLOCK = 64
ROPE_THETA = 500000.0
ROPE_FACTOR = 8.0
LOW_FACTOR = 1.0
HIGH_FACTOR = 4.0
TRAINED_CONTEXT = 8192.0
MASKED = -1e30
EXP2_SCALE = HEAD_DIM ** -0.5 * math.log2(math.e)
MESH = pl.DeviceIdType.MESH


def rope_tables(positions):
    half = HEAD_DIM // 2
    base = ROPE_THETA ** -(np.arange(half, dtype=np.float64) * 2.0 / HEAD_DIM)
    wavelength = 2.0 * np.pi / base
    smooth = (TRAINED_CONTEXT / wavelength - LOW_FACTOR) / (HIGH_FACTOR - LOW_FACTOR)
    blended = (1.0 - smooth) * base / ROPE_FACTOR + smooth * base
    frequency = np.where(
        wavelength < TRAINED_CONTEXT / HIGH_FACTOR,
        base,
        np.where(wavelength > TRAINED_CONTEXT / LOW_FACTOR, base / ROPE_FACTOR, blended),
    )
    angles = positions.astype(np.float64)[:, None] * frequency[None, :]
    cosine = np.concatenate([np.cos(angles), np.cos(angles)], axis=1)
    sine = np.concatenate([-np.sin(angles), np.sin(angles)], axis=1)
    return cosine.astype(np.float32), sine.astype(np.float32)


def flip(index, step, size):
    result, bit = 0, 1
    while bit < size:
        result = result + ((index // bit) % 2 + (step // bit) % 2) % 2 * bit
        bit *= 2
    return result


def kernel(
    n_seg, n_ctx,
    offsets_ref, q_ref, k_ref, v_ref, vert_ref, slash_ref, cos_ref, sin_ref, ocos_ref, osin_ref,
    out_ref,
    kv, qt, bias_tab, peak, total, numer,
    send_z, send_x, send_sib, recv,
):
    seg, ctx, head = lax.axis_index("seg"), lax.axis_index("ctx"), lax.axis_index("head")
    rows, heads = q_ref.shape[0], q_ref.shape[1] // HEAD_DIM
    keys = k_ref.shape[0]
    prefix = keys * n_seg * n_ctx - rows * n_ctx
    other = 1 - head
    own = seg * n_ctx + ctx

    def shard(t, u):
        return flip(seg, t, n_seg) * n_ctx + flip(ctx, u, n_ctx)

    barrier = pltpu.get_barrier_semaphore()
    for t in range(1, n_seg):
        pl.semaphore_signal(
            barrier, inc=1, device_id={"seg": flip(seg, t, n_seg)}, device_id_type=MESH
        )
    for u in range(1, n_ctx):
        pl.semaphore_signal(
            barrier, inc=1, device_id={"ctx": flip(ctx, u, n_ctx)}, device_id_type=MESH
        )
    pl.semaphore_signal(barrier, inc=1, device_id={"head": other}, device_id_type=MESH)

    def rotation(index):
        ocos = ocos_ref[pl.ds(index, 1), :]
        osin = osin_ref[pl.ds(index, 1), :]
        cosine = ocos * cos_ref[...] - osin * sin_ref[...]
        sine = osin * cos_ref[...] + ocos * sin_ref[...]
        return cosine, sine

    def rotate(x, cosine, sine):
        x = x.astype(jnp.float32)
        return x * cosine + pltpu.roll(x, HEAD_DIM // 2, 1) * sine

    cosine, sine = rotation(offsets_ref[own] // keys)
    kv[0, own] = rotate(k_ref[...], cosine, sine).astype(jnp.bfloat16)
    kv[1, own] = v_ref[...]

    pl.semaphore_wait(barrier, n_seg + n_ctx - 1)

    def copy_z(t):
        return pltpu.make_async_remote_copy(
            src_ref=kv.at[head, own], dst_ref=kv.at[head, own],
            send_sem=send_z.at[t], recv_sem=recv.at[head, own],
            device_id={"seg": flip(seg, t, n_seg)}, device_id_type=MESH,
        )

    def copy_x(t, u):
        index = shard(t, 0)
        return pltpu.make_async_remote_copy(
            src_ref=kv.at[head, index], dst_ref=kv.at[head, index],
            send_sem=send_x.at[t, u], recv_sem=recv.at[head, index],
            device_id={"ctx": flip(ctx, u, n_ctx)}, device_id_type=MESH,
        )

    def copy_sib(t, u):
        index = shard(t, u)
        return pltpu.make_async_remote_copy(
            src_ref=kv.at[head, index], dst_ref=kv.at[head, index],
            send_sem=send_sib.at[t, u], recv_sem=recv.at[head, index],
            device_id={"head": other}, device_id_type=MESH,
        )

    def arrived(kind, index):
        pltpu.make_async_remote_copy(
            src_ref=kv.at[kind, index], dst_ref=kv.at[kind, index],
            send_sem=send_z.at[0], recv_sem=recv.at[kind, index],
            device_id={"head": other}, device_id_type=MESH,
        ).wait_recv()

    for u in range(1, n_ctx):
        copy_x(0, u).start()
    for t in range(1, n_seg):
        copy_z(t).start()

    cosine, sine = rotation((prefix + ctx * rows) // keys)
    for h in range(heads):
        x = q_ref[:, h * HEAD_DIM : (h + 1) * HEAD_DIM]
        qt[:, h * rows : (h + 1) * rows] = rotate(x, cosine, sine).T.astype(jnp.bfloat16)

    lists, blocks = vert_ref.shape[0], bias_tab.shape[0]
    block_id = lax.broadcasted_iota(jnp.int32, (lists, blocks), 1)
    from_slash = (
        prefix // BLOCK + lax.broadcasted_iota(jnp.int32, slash_ref.shape, 0) - slash_ref[...]
    )
    vertical = vert_ref[...]
    hit = vertical[:, 0:1] == block_id
    for i in range(1, vertical.shape[1]):
        hit = hit | (vertical[:, i : i + 1] == block_id)
    for i in range(from_slash.shape[1]):
        hit = hit | (from_slash[:, i : i + 1] == block_id)
    list_id = lax.broadcasted_iota(jnp.int32, (lists, rows), 0)
    token_list = ctx * (rows // BLOCK) + lax.broadcasted_iota(jnp.int32, (lists, rows), 1) // BLOCK
    pick = jnp.where(list_id == token_list, 1.0, 0.0)
    spread = lax.dot_general(
        jnp.where(hit, 1.0, 0.0).T, pick, (((1,), (0,)), ((), ())),
        preferred_element_type=jnp.float32,
    )
    bias_tab[...] = jnp.where(spread > 0.5, 0.0, MASKED)

    lead = (
        prefix + ctx * rows
        + lax.broadcasted_iota(jnp.int32, (BLOCK, rows), 1)
        - lax.broadcasted_iota(jnp.int32, (BLOCK, rows), 0)
    )

    def attend(index, first=False):
        offset = offsets_ref[index]
        pieces = []
        for i in range(keys // BLOCK):
            row = bias_tab[pl.ds(offset // BLOCK + i, 1), :]
            pieces.append(jnp.where(lead >= offset + i * BLOCK, row, MASKED))
        bias = jnp.concatenate(pieces, axis=0)
        key_tile = kv[0, index]
        value_tile = kv[1, index].T
        for h in range(heads):
            columns = slice(h * rows, (h + 1) * rows)
            scores = (
                jnp.dot(key_tile, qt[:, columns], preferred_element_type=jnp.float32) + bias
            )
            fresh = jnp.max(scores, axis=0, keepdims=True)
            if not first:
                old = peak[:, columns]
                fresh = jnp.maximum(old, fresh)
            weights = jnp.exp2((scores - fresh) * EXP2_SCALE)
            added = jnp.sum(weights, axis=0, keepdims=True)
            product = jnp.dot(
                value_tile, weights.astype(jnp.bfloat16), preferred_element_type=jnp.float32
            )
            if not first:
                rescale = jnp.exp2((old - fresh) * EXP2_SCALE)
                added = added + total[:, columns] * rescale
                product = product + numer[:, columns] * rescale
            peak[:, columns] = fresh
            total[:, columns] = added
            numer[:, columns] = product

    attend(own, True)

    def across(t):
        for u in range(1, n_ctx):
            arrived(head, shard(t, u))
            copy_sib(t, u).start()

    def attend_across(t):
        for u in range(1, n_ctx):
            arrived(other, shard(t, u))
            attend(shard(t, u))

    def step(t, carry):
        arrived(head, shard(t, 0))
        for u in range(1, n_ctx):
            copy_x(t, u).start()
        copy_sib(t, 0).start()
        across(t - 1)
        attend_across(t - 1)
        arrived(other, shard(t, 0))
        attend(shard(t, 0))
        return carry

    lax.fori_loop(1, n_seg, step, 0)
    across(n_seg - 1)
    attend_across(n_seg - 1)

    for h in range(heads):
        columns = slice(h * rows, (h + 1) * rows)
        out_ref[:, h * HEAD_DIM : (h + 1) * HEAD_DIM] = (
            (numer[:, columns] / total[:, columns]).T.astype(jnp.bfloat16)
        )

    for t in range(1, n_seg):
        copy_z(t).wait_send()
        copy_sib(t, 0).wait_send()
    for t in range(n_seg):
        for u in range(1, n_ctx):
            copy_x(t, u).wait_send()
            copy_sib(t, u).wait_send()


def solution(mesh):
    n_seg, n_ctx = mesh.shape["seg"], mesh.shape["ctx"]

    def local(queries, cached_keys, cached_values, key_offsets, vertical_blocks, slash_offsets):
        rows, columns = queries.shape
        heads = columns // HEAD_DIM
        keys = cached_keys.shape[0]
        shards = n_seg * n_ctx
        blocks = -(-(keys * shards // BLOCK) // 128) * 128
        cosine, sine = rope_tables(np.arange(keys))
        ocos, osin = rope_tables(np.arange(shards) * keys)
        vmem = pl.BlockSpec(memory_space=pltpu.VMEM)
        smem = pl.BlockSpec(memory_space=pltpu.SMEM)
        return pl.pallas_call(
            functools.partial(kernel, n_seg, n_ctx),
            out_shape=jax.ShapeDtypeStruct((rows, columns), jnp.bfloat16),
            in_specs=[smem] + [vmem] * 9,
            out_specs=vmem,
            scratch_shapes=[
                pltpu.VMEM((2, shards, keys, HEAD_DIM), jnp.bfloat16),
                pltpu.VMEM((HEAD_DIM, heads * rows), jnp.bfloat16),
                pltpu.VMEM((blocks, rows), jnp.float32),
                pltpu.VMEM((1, heads * rows), jnp.float32),
                pltpu.VMEM((1, heads * rows), jnp.float32),
                pltpu.VMEM((HEAD_DIM, heads * rows), jnp.float32),
                pltpu.SemaphoreType.DMA((n_seg,)),
                pltpu.SemaphoreType.DMA((n_seg, n_ctx)),
                pltpu.SemaphoreType.DMA((n_seg, n_ctx)),
                pltpu.SemaphoreType.DMA((2, shards)),
            ],
            compiler_params=pltpu.CompilerParams(
                collective_id=0, has_side_effects=True, vmem_limit_bytes=48 * 1024 * 1024
            ),
        )(
            key_offsets, queries, cached_keys, cached_values, vertical_blocks, slash_offsets,
            cosine, sine, ocos, osin,
        )

    return jax.shard_map(
        local,
        mesh=mesh,
        in_specs=(
            P(("groups", "ctx"), "head"),
            P(("groups", "seg", "ctx"), None),
            P(("groups", "seg", "ctx"), None),
            P("groups"),
            P("groups", None),
            P("groups", None),
        ),
        out_specs=P(("groups", "ctx"), "head"),
        check_vma=False,
    )
```

time: 85.4 us -> 31.7 us (0.37); the launches traced: 84 us -> 31.2 us
  blocking collectives: 27.7 us -> 0 us
  Pallas kernels: 0 us -> 22.6 us
  other arithmetic: 16.5 us -> 0 us
  between operations: 15 us -> 0.02 us
  waiting for transfers between devices: 11.8 us -> 0 us
  matrix products: 2.3 us -> 0 us
  local copies, waits for them, and re-layouts: 10.6 us -> 8.54 us
    all_gather x4 -> x0, blocking collectives: 27.7 us -> none  [the longest x2 19.6 us: combined_all(): lax.all_gather(a.astype(kind), axis)]
    pallas_call x0 -> x1, Pallas kernels: none -> 22.6 us  [local(): pl.pallas_call(functools.partial(kernel, n_seg, n_ctx), out_shape=jax.Sha...]
    all_gather x1 -> x0, waiting for transfers between devices: 11.7 us -> none  [combined_all(): lax.all_gather(a.astype(kind), axis)]
    add x10 -> x0, other arithmetic: 5.79 us -> none  [the longest x3 4.38 us: combine_partials(): earlier[1] * earlier_scale[:, None] + later[1] * later_scale[:, None]]
    unnamed x20 -> x21, local copies, waits for them, and re-layouts: 4.68 us -> 8.54 us
    convert_element_type x14 -> x0, other arithmetic: 3.71 us -> none  [the longest x3 1.42 us: combined_all(): a.astype(kind)]
    reduce_or x4 -> x0, other arithmetic: 2.57 us -> none  [the longest x2 2.35 us: attend_keys(): result = lax.cond(jnp.any(tile_mask), update, unchanged, current)]
    dot_general x4 -> x0, matrix products: 2.3 us -> none  [the longest x2 1.63 us: update(): jnp.dot(weights.astype(jnp.bfloat16), value_tile, preferred_element_type=...]
  transfers between devices with their start and end apart: 1 -> 0, of which waited for: 1 -> 0; matrix products, arithmetic and copies ran while one was open for 1% -> 0% of each run, Pallas kernels for 0% -> 0%
where the time goes in v1:
time: 31.7 us; the launch traced here: 31.2 us
  Pallas kernels  22.6 us (71%)
  local copies, waits for them, and re-layouts  8.54 us (27%)
    pallas_call x1, Pallas kernels, local(): pl.pallas_call(functools.partial(kernel, n_seg, n_ctx), out_shape=jax.Sha...  22.6 us
    unnamed x21, local copies, waits for them, and re-layouts  8.54 us

profile of v1, /device:TPU:1, one launch (start us, length us, event | category | flops | bytes accessed | tf_op | source)
XLA Modules:
  0.0 31.2 jit_solution(9995981800881479824)
XLA Ops:
  0.0 0.0 copy-start.7
  0.0 0.7 %copy-done.7 = f32[8,128]{1,0:T(8,128)S(1)} copy-done((f32[8,128]{1,0:T(8,128)S(1)}, f32[8,128]{1,0:T(8,128)}, u32[]{:S(2)}) %copy-start.7) | copy-done | bytes 4120
  0.7 0.0 copy-start
  0.7 0.9 %copy-done = bf16[256,512]{1,0:T(8,128)(2,1)S(1)} copy-done((bf16[256,512]{1,0:T(8,128)(2,1)S(1)}, bf16[256,512]{1,0:T(8,128)(2,1)}, u32[]{:S(2)}) %copy-start) | copy-done | bytes 262168
  1.6 0.0 copy-start.1
  1.6 0.9 %copy-done.1 = f32[256,128]{1,0:T(8,128)S(1)} copy-done((f32[256,128]{1,0:T(8,128)S(1)}, f32[256,128]{1,0:T(8,128)}, u32[]{:S(2)}) %copy-start.1) | copy-done | bytes 131096
  2.5 0.0 copy-start.2
  2.5 0.9 %copy-done.2 = f32[256,128]{1,0:T(8,128)S(1)} copy-done((f32[256,128]{1,0:T(8,128)S(1)}, f32[256,128]{1,0:T(8,128)}, u32[]{:S(2)}) %copy-start.2) | copy-done | bytes 131096
  3.4 0.0 copy-start.3
  3.5 0.8 %copy-done.3 = bf16[256,128]{1,0:T(8,128)(2,1)S(1)} copy-done((bf16[256,128]{1,0:T(8,128)(2,1)S(1)}, bf16[256,128]{1,0:T(8,128)(2,1)}, u32[]{:S(2)}) %copy-start.3) | copy-done | bytes 65560
  4.3 0.0 copy-start.4
  4.3 0.8 %copy-done.4 = bf16[256,128]{1,0:T(8,128)(2,1)S(1)} copy-done((bf16[256,128]{1,0:T(8,128)(2,1)S(1)}, bf16[256,128]{1,0:T(8,128)(2,1)}, u32[]{:S(2)}) %copy-start.4) | copy-done | bytes 65560
  5.1 0.0 copy-start.5
  5.1 0.7 %copy-done.5 = s32[8,16]{1,0:T(8,128)S(1)} copy-done((s32[8,16]{1,0:T(8,128)S(1)}, s32[8,16]{1,0:T(8,128)}, u32[]{:S(2)}) %copy-start.5) | copy-done | bytes 536
  5.8 0.0 copy-start.6
  5.8 0.7 %copy-done.6 = s32[8,32]{1,0:T(8,128)S(1)} copy-done((s32[8,32]{1,0:T(8,128)S(1)}, s32[8,32]{1,0:T(8,128)}, u32[]{:S(2)}) %copy-start.6) | copy-done | bytes 1048
  6.5 0.0 copy-start.8
  6.5 0.7 %copy-done.8 = f32[8,128]{1,0:T(8,128)S(1)} copy-done((f32[8,128]{1,0:T(8,128)S(1)}, f32[8,128]{1,0:T(8,128)}, u32[]{:S(2)}) %copy-start.8) | copy-done | bytes 4120
  7.2 0.0 copy-start.9
  7.2 0.7 %copy-done.9 = s32[8]{0:T(128)S(1)} copy-done((s32[8]{0:T(128)S(1)}, s32[8]{0:T(128)}, u32[]{:S(2)}) %copy-start.9) | copy-done | bytes 56
  7.8 22.6 %shard_map.100 = bf16[256,512]{1,0:T(8,128)(2,1)S(1)} custom-call(s32[8]{0:T(128)S(1)} %copy-done.9, bf16[256,512]{1,0:T(8,128)(2,1)S(1)} %copy-done, bf16[256,128]{1,0:T(8,128)(2,1)S(1)} %copy-done.3, bf16[256,128]{1,0:T(8,128)(2,1)S(1)} %copy-done.4, s32[8,16]{1,0:T(8,128)S(1)} %copy-done.5, s32[8,32]{1,0:T(8,128)S(1)} %copy-done.6, ...), custom_call_target="tpu_custom_call" | custom-call | tf_op jit(solution)/shard_map/pallas_call | solution.py:246
  30.5 0.7 %copy.12 = bf16[256,512]{1,0:T(8,128)(2,1)} copy(bf16[256,512]{1,0:T(8,128)(2,1)S(1)} %shard_map.100) | data formatting | bytes 524288
Async XLA Ops:
  0.0 0.7 %copy-start.7 = (f32[8,128]{1,0:T(8,128)S(1)}, f32[8,128]{1,0:T(8,128)}, u32[]{:S(2)}) copy-start(f32[8,128]{1,0:T(8,128)} %constant.11.clone.osin_ref) | copy-start | bytes 12292
  0.7 0.9 %copy-start = (bf16[256,512]{1,0:T(8,128)(2,1)S(1)}, bf16[256,512]{1,0:T(8,128)(2,1)}, u32[]{:S(2)}) copy-start(bf16[256,512]{1,0:T(8,128)(2,1)} %q_ref.1) | copy-start | bytes 786436
  1.6 0.9 %copy-start.1 = (f32[256,128]{1,0:T(8,128)S(1)}, f32[256,128]{1,0:T(8,128)}, u32[]{:S(2)}) copy-start(f32[256,128]{1,0:T(8,128)} %constant.9.clone.sin_ref) | copy-start | bytes 393220
  2.5 0.9 %copy-start.2 = (f32[256,128]{1,0:T(8,128)S(1)}, f32[256,128]{1,0:T(8,128)}, u32[]{:S(2)}) copy-start(f32[256,128]{1,0:T(8,128)} %constant.8.clone.cos_ref) | copy-start | bytes 393220
  3.4 0.8 %copy-start.3 = (bf16[256,128]{1,0:T(8,128)(2,1)S(1)}, bf16[256,128]{1,0:T(8,128)(2,1)}, u32[]{:S(2)}) copy-start(bf16[256,128]{1,0:T(8,128)(2,1)} %k_ref.1) | copy-start | bytes 196612
  4.3 0.8 %copy-start.4 = (bf16[256,128]{1,0:T(8,128)(2,1)S(1)}, bf16[256,128]{1,0:T(8,128)(2,1)}, u32[]{:S(2)}) copy-start(bf16[256,128]{1,0:T(8,128)(2,1)} %v_ref.1) | copy-start | bytes 196612
  5.1 0.7 %copy-start.5 = (s32[8,16]{1,0:T(8,128)S(1)}, s32[8,16]{1,0:T(8,128)}, u32[]{:S(2)}) copy-start(s32[8,16]{1,0:T(8,128)} %vert_ref.1) | copy-start | bytes 1540
  5.8 0.7 %copy-start.6 = (s32[8,32]{1,0:T(8,128)S(1)}, s32[8,32]{1,0:T(8,128)}, u32[]{:S(2)}) copy-start(s32[8,32]{1,0:T(8,128)} %slash_ref.1) | copy-start | bytes 3076
  6.5 0.7 %copy-start.8 = (f32[8,128]{1,0:T(8,128)S(1)}, f32[8,128]{1,0:T(8,128)}, u32[]{:S(2)}) copy-start(f32[8,128]{1,0:T(8,128)} %constant.10.clone.ocos_ref) | copy-start | bytes 12292
  7.2 0.7 %copy-start.9 = (s32[8]{0:T(128)S(1)}, s32[8]{0:T(128)}, u32[]{:S(2)}) copy-start(s32[8]{0:T(128)} %offsets_ref.1) | copy-start | bytes 100

commit v2 on v1

--- a/solution.py
+++ b/solution.py
@@ -48,10 +48,11 @@
 
 def kernel(
     n_seg, n_ctx,
-    offsets_ref, q_ref, k_ref, v_ref, vert_ref, slash_ref, cos_ref, sin_ref, ocos_ref, osin_ref,
+    offsets_hbm, q_hbm, k_hbm, v_hbm, vert_hbm, slash_hbm, table_hbm, start_hbm,
     out_ref,
+    offsets_ref, q_ref, k_ref, vert_ref, slash_ref, table_ref, start_ref,
     kv, qt, bias_tab, peak, total, numer,
-    send_z, send_x, send_sib, recv,
+    load, send_z, send_x, send_sib, recv,
 ):
     seg, ctx, head = lax.axis_index("seg"), lax.axis_index("ctx"), lax.axis_index("head")
     rows, heads = q_ref.shape[0], q_ref.shape[1] // HEAD_DIM
@@ -63,6 +64,22 @@
     def shard(t, u):
         return flip(seg, t, n_seg) * n_ctx + flip(ctx, u, n_ctx)
 
+    loads = [
+        pltpu.make_async_copy(source, target, load.at[i])
+        for i, (source, target) in enumerate((
+            (offsets_hbm, offsets_ref),
+            (start_hbm, start_ref),
+            (k_hbm, k_ref),
+            (table_hbm, table_ref),
+            (v_hbm, kv.at[1, own]),
+            (q_hbm, q_ref),
+            (vert_hbm, vert_ref),
+            (slash_hbm, slash_ref),
+        ))
+    ]
+    for copy in loads:
+        copy.start()
+
     barrier = pltpu.get_barrier_semaphore()
     for t in range(1, n_seg):
         pl.semaphore_signal(
@@ -75,19 +92,21 @@
     pl.semaphore_signal(barrier, inc=1, device_id={"head": other}, device_id_type=MESH)
 
     def rotation(index):
-        ocos = ocos_ref[pl.ds(index, 1), :]
-        osin = osin_ref[pl.ds(index, 1), :]
-        cosine = ocos * cos_ref[...] - osin * sin_ref[...]
-        sine = osin * cos_ref[...] + ocos * sin_ref[...]
+        ocos = start_ref[0, pl.ds(index, 1), :]
+        osin = start_ref[1, pl.ds(index, 1), :]
+        cosine = ocos * table_ref[0] - osin * table_ref[1]
+        sine = osin * table_ref[0] + ocos * table_ref[1]
         return cosine, sine
 
     def rotate(x, cosine, sine):
         x = x.astype(jnp.float32)
         return x * cosine + pltpu.roll(x, HEAD_DIM // 2, 1) * sine
 
+    for copy in loads[:4]:
+        copy.wait()
     cosine, sine = rotation(offsets_ref[own] // keys)
     kv[0, own] = rotate(k_ref[...], cosine, sine).astype(jnp.bfloat16)
-    kv[1, own] = v_ref[...]
+    loads[4].wait()
 
     pl.semaphore_wait(barrier, n_seg + n_ctx - 1)
 
@@ -126,6 +145,8 @@
     for t in range(1, n_seg):
         copy_z(t).start()
 
+    for copy in loads[5:]:
+        copy.wait()
     cosine, sine = rotation((prefix + ctx * rows) // keys)
     for h in range(heads):
         x = q_ref[:, h * HEAD_DIM : (h + 1) * HEAD_DIM]
@@ -239,34 +260,41 @@
         keys = cached_keys.shape[0]
         shards = n_seg * n_ctx
         blocks = -(-(keys * shards // BLOCK) // 128) * 128
-        cosine, sine = rope_tables(np.arange(keys))
-        ocos, osin = rope_tables(np.arange(shards) * keys)
-        vmem = pl.BlockSpec(memory_space=pltpu.VMEM)
-        smem = pl.BlockSpec(memory_space=pltpu.SMEM)
+        table = np.stack(rope_tables(np.arange(keys)))
+        start = np.stack(rope_tables(np.arange(shards) * keys))
+        operands = (
+            key_offsets, queries, cached_keys, cached_values, vertical_blocks, slash_offsets,
+            table, start,
+        )
         return pl.pallas_call(
             functools.partial(kernel, n_seg, n_ctx),
             out_shape=jax.ShapeDtypeStruct((rows, columns), jnp.bfloat16),
-            in_specs=[smem] + [vmem] * 9,
-            out_specs=vmem,
+            in_specs=[pl.BlockSpec(memory_space=pltpu.HBM)] * len(operands),
+            out_specs=pl.BlockSpec(memory_space=pltpu.VMEM),
             scratch_shapes=[
+                pltpu.SMEM(key_offsets.shape, jnp.int32),
+                pltpu.VMEM(queries.shape, jnp.bfloat16),
+                pltpu.VMEM(cached_keys.shape, jnp.bfloat16),
+                pltpu.VMEM(vertical_blocks.shape, jnp.int32),
+                pltpu.VMEM(slash_offsets.shape, jnp.int32),
+                pltpu.VMEM(table.shape, jnp.float32),
+                pltpu.VMEM(start.shape, jnp.float32),
                 pltpu.VMEM((2, shards, keys, HEAD_DIM), jnp.bfloat16),
                 pltpu.VMEM((HEAD_DIM, heads * rows), jnp.bfloat16),
                 pltpu.VMEM((blocks, rows), jnp.float32),
                 pltpu.VMEM((1, heads * rows), jnp.float32),
                 pltpu.VMEM((1, heads * rows), jnp.float32),
                 pltpu.VMEM((HEAD_DIM, heads * rows), jnp.float32),
+                pltpu.SemaphoreType.DMA((len(operands),)),
                 pltpu.SemaphoreType.DMA((n_seg,)),
                 pltpu.SemaphoreType.DMA((n_seg, n_ctx)),
                 pltpu.SemaphoreType.DMA((n_seg, n_ctx)),
                 pltpu.SemaphoreType.DMA((2, shards)),
             ],
             compiler_params=pltpu.CompilerParams(
-                collective_id=0, has_side_effects=True, vmem_limit_bytes=48 * 1024 * 1024
+                collective_id=0, has_side_effects=True, vmem_limit_bytes=63 * 1024 * 1024
             ),
-        )(
-            key_offsets, queries, cached_keys, cached_values, vertical_blocks, slash_offsets,
-            cosine, sine, ocos, osin,
-        )
+        )(*operands)
 
     return jax.shard_map(
         local,

time: 31.7 us -> 24.8 us (0.78); the launches traced: 31.2 us -> 24.6 us
  local copies, waits for them, and re-layouts: 8.54 us -> 1.67 us
  Pallas kernels: 22.6 us -> 23 us
    unnamed x21 -> x1, local copies, waits for them, and re-layouts: 8.54 us -> 1.67 us
    pallas_call x1, Pallas kernels: 22.6 us -> 23 us  [local(): pl.pallas_call(functools.partial(kernel, n_seg, n_ctx), out_shape=jax.Sha...]
where the time goes in v2:
time: 24.8 us; the launch traced here: 24.6 us
  Pallas kernels  23 us (93%)
  local copies, waits for them, and re-layouts  1.67 us (7%)
    pallas_call x1, Pallas kernels, local(): pl.pallas_call(functools.partial(kernel, n_seg, n_ctx), out_shape=jax.Sha...  23 us
    unnamed x1, local copies, waits for them, and re-layouts  1.67 us

profile of v2, /device:TPU:1, one launch (start us, length us, event | category | flops | bytes accessed | tf_op | source)
XLA Modules:
  0.0 24.6 jit_solution(7619892117086114888)
XLA Ops:
  0.0 23.0 %shard_map.82 = bf16[256,512]{1,0:T(8,128)(2,1)} custom-call(s32[8]{0:T(128)} %offsets_hbm.1, bf16[256,512]{1,0:T(8,128)(2,1)} %q_hbm.1, bf16[256,128]{1,0:T(8,128)(2,1)} %k_hbm.1, bf16[256,128]{1,0:T(8,128)(2,1)} %v_hbm.1, s32[8,16]{1,0:T(8,128)} %vert_hbm.1, s32[8,32]{1,0:T(8,128)} %slash_hbm.1, f32[2,256,128]{2,1,0:T(8,128)} %constant.4.clone.table_hbm, ...), custom_call_target="tpu_custom_call" | custom-call | tf_op jit(solution)/shard_map/pallas_call | solution.py:269
  23.0 1.7 %copy.10 = bf16[256,512]{1,0:T(8,128)(2,1)} copy(bf16[256,512]{1,0:T(8,128)(2,1)} %shard_map.82) | data formatting | bytes 524288

commit v3 on v2

--- a/solution.py
+++ b/solution.py
@@ -51,7 +51,7 @@
     offsets_hbm, q_hbm, k_hbm, v_hbm, vert_hbm, slash_hbm, table_hbm, start_hbm,
     out_ref,
     offsets_ref, q_ref, k_ref, vert_ref, slash_ref, table_ref, start_ref,
-    kv, qt, bias_tab, peak, total, numer,
+    kv, qt, bias_tab, peak, total, numer, held,
     load, send_z, send_x, send_sib, recv,
 ):
     seg, ctx, head = lax.axis_index("seg"), lax.axis_index("ctx"), lax.axis_index("head")
@@ -187,27 +187,31 @@
         bias = jnp.concatenate(pieces, axis=0)
         key_tile = kv[0, index]
         value_tile = kv[1, index].T
-        for h in range(heads):
-            columns = slice(h * rows, (h + 1) * rows)
+        spans = [slice(h * rows, (h + 1) * rows) for h in range(heads)]
+        fresh, old = [], []
+        for columns in spans:
             scores = (
                 jnp.dot(key_tile, qt[:, columns], preferred_element_type=jnp.float32) + bias
             )
-            fresh = jnp.max(scores, axis=0, keepdims=True)
-            if not first:
-                old = peak[:, columns]
-                fresh = jnp.maximum(old, fresh)
-            weights = jnp.exp2((scores - fresh) * EXP2_SCALE)
+            held[:, columns] = scores
+            fresh.append(jnp.max(scores, axis=0, keepdims=True))
+        if not first:
+            old = [peak[:, columns] for columns in spans]
+            fresh = [jnp.maximum(a, b) for a, b in zip(old, fresh)]
+        for h, columns in enumerate(spans):
+            weights = jnp.exp2((held[:, columns] - fresh[h]) * EXP2_SCALE)
             added = jnp.sum(weights, axis=0, keepdims=True)
             product = jnp.dot(
                 value_tile, weights.astype(jnp.bfloat16), preferred_element_type=jnp.float32
             )
             if not first:
-                rescale = jnp.exp2((old - fresh) * EXP2_SCALE)
+                rescale = jnp.exp2((old[h] - fresh[h]) * EXP2_SCALE)
                 added = added + total[:, columns] * rescale
                 product = product + numer[:, columns] * rescale
-            peak[:, columns] = fresh
             total[:, columns] = added
             numer[:, columns] = product
+        for h, columns in enumerate(spans):
+            peak[:, columns] = fresh[h]
 
     attend(own, True)
 
@@ -285,6 +289,7 @@
                 pltpu.VMEM((1, heads * rows), jnp.float32),
                 pltpu.VMEM((1, heads * rows), jnp.float32),
                 pltpu.VMEM((HEAD_DIM, heads * rows), jnp.float32),
+                pltpu.VMEM((keys, heads * rows), jnp.float32),
                 pltpu.SemaphoreType.DMA((len(operands),)),
                 pltpu.SemaphoreType.DMA((n_seg,)),
                 pltpu.SemaphoreType.DMA((n_seg, n_ctx)),

time: 24.8 us -> 22.1 us (0.89)
  Pallas kernels: 23 us -> 20.2 us
    pallas_call x1, Pallas kernels: 23 us -> 20.2 us  [local(): pl.pallas_call(functools.partial(kernel, n_seg, n_ctx), out_shape=jax.Sha...]
where the time goes in v3:
time: 22.1 us; the launch traced here: 21.9 us
  Pallas kernels  20.2 us (91%)
  local copies, waits for them, and re-layouts  1.67 us (8%)
    pallas_call x1, Pallas kernels, local(): pl.pallas_call(functools.partial(kernel, n_seg, n_ctx), out_shape=jax.Sha...  20.2 us
    unnamed x1, local copies, waits for them, and re-layouts  1.67 us

profile of v3, /device:TPU:1, one launch (start us, length us, event | category | flops | bytes accessed | tf_op | source)
XLA Modules:
  0.0 21.9 jit_solution(3055198389786473679)
XLA Ops:
  0.0 20.2 %shard_map.82 = bf16[256,512]{1,0:T(8,128)(2,1)} custom-call(s32[8]{0:T(128)} %offsets_hbm.1, bf16[256,512]{1,0:T(8,128)(2,1)} %q_hbm.1, bf16[256,128]{1,0:T(8,128)(2,1)} %k_hbm.1, bf16[256,128]{1,0:T(8,128)(2,1)} %v_hbm.1, s32[8,16]{1,0:T(8,128)} %vert_hbm.1, s32[8,32]{1,0:T(8,128)} %slash_hbm.1, f32[2,256,128]{2,1,0:T(8,128)} %constant.4.clone.table_hbm, ...), custom_call_target="tpu_custom_call" | custom-call | tf_op jit(solution)/shard_map/pallas_call | solution.py:273
  20.2 1.7 %copy.10 = bf16[256,512]{1,0:T(8,128)(2,1)} copy(bf16[256,512]{1,0:T(8,128)(2,1)} %shard_map.82) | data formatting | bytes 524288

commit v4 on v3

--- a/solution.py
+++ b/solution.py
@@ -140,10 +140,10 @@
             device_id={"head": other}, device_id_type=MESH,
         ).wait_recv()
 
+    for t in range(1, n_seg):
+        copy_z(t).start()
     for u in range(1, n_ctx):
         copy_x(0, u).start()
-    for t in range(1, n_seg):
-        copy_z(t).start()
 
     for copy in loads[5:]:
         copy.wait()
@@ -225,19 +225,28 @@
             arrived(other, shard(t, u))
             attend(shard(t, u))
 
-    def step(t, carry):
+    def forward(t):
         arrived(head, shard(t, 0))
         for u in range(1, n_ctx):
             copy_x(t, u).start()
         copy_sib(t, 0).start()
         across(t - 1)
-        attend_across(t - 1)
+
+    def attend_along(t):
         arrived(other, shard(t, 0))
         attend(shard(t, 0))
+
+    def step(t, carry):
+        forward(t)
+        attend_along(t - 1)
+        attend_across(t - 2)
         return carry
 
-    lax.fori_loop(1, n_seg, step, 0)
+    forward(1)
+    lax.fori_loop(2, n_seg, step, 0)
+    attend_across(n_seg - 2)
     across(n_seg - 1)
+    attend_along(n_seg - 1)
     attend_across(n_seg - 1)
 
     for h in range(heads):

time: 22.1 us -> 21 us (0.950)
  Pallas kernels: 20.2 us -> 19.2 us
    pallas_call x1, Pallas kernels: 20.2 us -> 19.2 us  [local(): pl.pallas_call(functools.partial(kernel, n_seg, n_ctx), out_shape=jax.Sha...]
where the time goes in v4:
time: 21 us; the launch traced here: 20.9 us
  Pallas kernels  19.2 us (91%)
  local copies, waits for them, and re-layouts  1.67 us (8%)
    pallas_call x1, Pallas kernels, local(): pl.pallas_call(functools.partial(kernel, n_seg, n_ctx), out_shape=jax.Sha...  19.2 us
    unnamed x1, local copies, waits for them, and re-layouts  1.67 us

profile of v4, /device:TPU:1, one launch (start us, length us, event | category | flops | bytes accessed | tf_op | source)
XLA Modules:
  0.0 20.9 jit_solution(4482184495434588367)
XLA Ops:
  0.0 19.2 %shard_map.82 = bf16[256,512]{1,0:T(8,128)(2,1)} custom-call(s32[8]{0:T(128)} %offsets_hbm.1, bf16[256,512]{1,0:T(8,128)(2,1)} %q_hbm.1, bf16[256,128]{1,0:T(8,128)(2,1)} %k_hbm.1, bf16[256,128]{1,0:T(8,128)(2,1)} %v_hbm.1, s32[8,16]{1,0:T(8,128)} %vert_hbm.1, s32[8,32]{1,0:T(8,128)} %slash_hbm.1, f32[2,256,128]{2,1,0:T(8,128)} %constant.4.clone.table_hbm, ...), custom_call_target="tpu_custom_call" | custom-call | tf_op jit(solution)/shard_map/pallas_call | solution.py:282
  19.2 1.7 %copy.10 = bf16[256,512]{1,0:T(8,128)(2,1)} copy(bf16[256,512]{1,0:T(8,128)(2,1)} %shard_map.82) | data formatting | bytes 524288

commit v5 on v4

--- a/solution.py
+++ b/solution.py
@@ -306,9 +306,9 @@
                 pltpu.SemaphoreType.DMA((2, shards)),
             ],
             compiler_params=pltpu.CompilerParams(
-                collective_id=0, has_side_effects=True, vmem_limit_bytes=63 * 1024 * 1024
+                collective_id=0, has_side_effects=True, vmem_limit_bytes=48 * 1024 * 1024
             ),
-        )(*operands)
+        )(*(pltpu.with_memory_space_constraint(x, pltpu.HBM) for x in map(jnp.asarray, operands)))
 
     return jax.shard_map(
         local,

time: 21 us -> 19.4 us (0.924)
  local copies, waits for them, and re-layouts: 1.67 us -> 0.71 us
  Pallas kernels: 19.2 us -> 18.5 us
    unnamed x1, local copies, waits for them, and re-layouts: 1.67 us -> 0.71 us
    pallas_call x1, Pallas kernels: 19.2 us -> 18.5 us  [local(): pl.pallas_call(functools.partial(kernel, n_seg, n_ctx), out_shape=jax.Sha...]
where the time goes in v5:
time: 19.4 us; the launch traced here: 19.2 us
  Pallas kernels  18.5 us (95%)
  local copies, waits for them, and re-layouts  0.71 us (4%)
    pallas_call x1, Pallas kernels, local(): pl.pallas_call(functools.partial(kernel, n_seg, n_ctx), out_shape=jax.Sha...  18.5 us
    unnamed x1, local copies, waits for them, and re-layouts  0.71 us

profile of v5, /device:TPU:1, one launch (start us, length us, event | category | flops | bytes accessed | tf_op | source)
XLA Modules:
  0.0 19.2 jit_solution(8626838406075683944)
XLA Ops:
  0.0 18.5 %shard_map.82 = bf16[256,512]{1,0:T(8,128)(2,1)S(1)} custom-call(s32[8]{0:T(128)} %offsets_hbm.1, bf16[256,512]{1,0:T(8,128)(2,1)} %q_hbm.1, bf16[256,128]{1,0:T(8,128)(2,1)} %k_hbm.1, bf16[256,128]{1,0:T(8,128)(2,1)} %v_hbm.1, s32[8,16]{1,0:T(8,128)} %vert_hbm.1, s32[8,32]{1,0:T(8,128)} %slash_hbm.1, f32[2,256,128]{2,1,0:T(8,128)} %constant.4.clone.table_hbm, ...), custom_call_target="tpu_custom_call" | custom-call | tf_op jit(solution)/shard_map/pallas_call | solution.py:282
  18.5 0.7 %copy.10 = bf16[256,512]{1,0:T(8,128)(2,1)} copy(bf16[256,512]{1,0:T(8,128)(2,1)S(1)} %shard_map.82) | data formatting | bytes 524288

commit v6 on v5

--- a/solution.py
+++ b/solution.py
@@ -17,6 +17,7 @@
 HIGH_FACTOR = 4.0
 TRAINED_CONTEXT = 8192.0
 MASKED = -1e30
+PIECES = 2
 EXP2_SCALE = HEAD_DIM ** -0.5 * math.log2(math.e)
 MESH = pl.DeviceIdType.MESH
 
@@ -110,40 +111,45 @@
 
     pl.semaphore_wait(barrier, n_seg + n_ctx - 1)
 
-    def copy_z(t):
+    def piece(kind, index, p):
+        return kv.at[kind, index, pl.ds(p * (keys // PIECES), keys // PIECES)]
+
+    def copy_z(t, p):
         return pltpu.make_async_remote_copy(
-            src_ref=kv.at[head, own], dst_ref=kv.at[head, own],
-            send_sem=send_z.at[t], recv_sem=recv.at[head, own],
+            src_ref=piece(head, own, p), dst_ref=piece(head, own, p),
+            send_sem=send_z.at[t, p], recv_sem=recv.at[head, own, p],
             device_id={"seg": flip(seg, t, n_seg)}, device_id_type=MESH,
         )
 
-    def copy_x(t, u):
+    def copy_x(t, u, p):
         index = shard(t, 0)
         return pltpu.make_async_remote_copy(
-            src_ref=kv.at[head, index], dst_ref=kv.at[head, index],
-            send_sem=send_x.at[t, u], recv_sem=recv.at[head, index],
+            src_ref=piece(head, index, p), dst_ref=piece(head, index, p),
+            send_sem=send_x.at[t, u, p], recv_sem=recv.at[head, index, p],
             device_id={"ctx": flip(ctx, u, n_ctx)}, device_id_type=MESH,
         )
 
-    def copy_sib(t, u):
+    def copy_sib(t, u, p):
         index = shard(t, u)
         return pltpu.make_async_remote_copy(
-            src_ref=kv.at[head, index], dst_ref=kv.at[head, index],
-            send_sem=send_sib.at[t, u], recv_sem=recv.at[head, index],
+            src_ref=piece(head, index, p), dst_ref=piece(head, index, p),
+            send_sem=send_sib.at[t, u, p], recv_sem=recv.at[head, index, p],
             device_id={"head": other}, device_id_type=MESH,
         )
 
-    def arrived(kind, index):
+    def arrived(kind, index, p):
         pltpu.make_async_remote_copy(
-            src_ref=kv.at[kind, index], dst_ref=kv.at[kind, index],
-            send_sem=send_z.at[0], recv_sem=recv.at[kind, index],
+            src_ref=piece(kind, index, p), dst_ref=piece(kind, index, p),
+            send_sem=send_z.at[0, p], recv_sem=recv.at[kind, index, p],
             device_id={"head": other}, device_id_type=MESH,
         ).wait_recv()
 
     for t in range(1, n_seg):
-        copy_z(t).start()
+        for p in range(PIECES):
+            copy_z(t, p).start()
     for u in range(1, n_ctx):
-        copy_x(0, u).start()
+        for p in range(PIECES):
+            copy_x(0, u, p).start()
 
     for copy in loads[5:]:
         copy.wait()
@@ -217,23 +223,27 @@
 
     def across(t):
         for u in range(1, n_ctx):
-            arrived(head, shard(t, u))
-            copy_sib(t, u).start()
+            for p in range(PIECES):
+                arrived(head, shard(t, u), p)
+                copy_sib(t, u, p).start()
 
     def attend_across(t):
         for u in range(1, n_ctx):
-            arrived(other, shard(t, u))
+            for p in range(PIECES):
+                arrived(other, shard(t, u), p)
             attend(shard(t, u))
 
     def forward(t):
-        arrived(head, shard(t, 0))
-        for u in range(1, n_ctx):
-            copy_x(t, u).start()
-        copy_sib(t, 0).start()
+        for p in range(PIECES):
+            arrived(head, shard(t, 0), p)
+            for u in range(1, n_ctx):
+                copy_x(t, u, p).start()
+            copy_sib(t, 0, p).start()
         across(t - 1)
 
     def attend_along(t):
-        arrived(other, shard(t, 0))
+        for p in range(PIECES):
+            arrived(other, shard(t, 0), p)
         attend(shard(t, 0))
 
     def step(t, carry):
@@ -255,13 +265,14 @@
             (numer[:, columns] / total[:, columns]).T.astype(jnp.bfloat16)
         )
 
-    for t in range(1, n_seg):
-        copy_z(t).wait_send()
-        copy_sib(t, 0).wait_send()
-    for t in range(n_seg):
-        for u in range(1, n_ctx):
-            copy_x(t, u).wait_send()
-            copy_sib(t, u).wait_send()
+    for p in range(PIECES):
+        for t in range(1, n_seg):
+            copy_z(t, p).wait_send()
+            copy_sib(t, 0, p).wait_send()
+        for t in range(n_seg):
+            for u in range(1, n_ctx):
+                copy_x(t, u, p).wait_send()
+                copy_sib(t, u, p).wait_send()
 
 
 def solution(mesh):
@@ -300,10 +311,10 @@
                 pltpu.VMEM((HEAD_DIM, heads * rows), jnp.float32),
                 pltpu.VMEM((keys, heads * rows), jnp.float32),
                 pltpu.SemaphoreType.DMA((len(operands),)),
-                pltpu.SemaphoreType.DMA((n_seg,)),
-                pltpu.SemaphoreType.DMA((n_seg, n_ctx)),
-                pltpu.SemaphoreType.DMA((n_seg, n_ctx)),
-                pltpu.SemaphoreType.DMA((2, shards)),
+                pltpu.SemaphoreType.DMA((n_seg, PIECES)),
+                pltpu.SemaphoreType.DMA((n_seg, n_ctx, PIECES)),
+                pltpu.SemaphoreType.DMA((n_seg, n_ctx, PIECES)),
+                pltpu.SemaphoreType.DMA((2, shards, PIECES)),
             ],
             compiler_params=pltpu.CompilerParams(
                 collective_id=0, has_side_effects=True, vmem_limit_bytes=48 * 1024 * 1024

time: 19.4 us -> 19.3 us (level)
  no operation moved by 1% of the time
where the time goes in v6:
time: 19.3 us; the launch traced here: 19.2 us
  Pallas kernels  18.4 us (95%)
  local copies, waits for them, and re-layouts  0.71 us (4%)
    pallas_call x1, Pallas kernels, local(): pl.pallas_call(functools.partial(kernel, n_seg, n_ctx), out_shape=jax.Sha...  18.4 us
    unnamed x1, local copies, waits for them, and re-layouts  0.71 us

profile of v6, /device:TPU:1, one launch (start us, length us, event | category | flops | bytes accessed | tf_op | source)
XLA Modules:
  0.0 19.2 jit_solution(7508911092202510421)
XLA Ops:
  0.0 18.4 %shard_map.82 = bf16[256,512]{1,0:T(8,128)(2,1)S(1)} custom-call(s32[8]{0:T(128)} %offsets_hbm.1, bf16[256,512]{1,0:T(8,128)(2,1)} %q_hbm.1, bf16[256,128]{1,0:T(8,128)(2,1)} %k_hbm.1, bf16[256,128]{1,0:T(8,128)(2,1)} %v_hbm.1, s32[8,16]{1,0:T(8,128)} %vert_hbm.1, s32[8,32]{1,0:T(8,128)} %slash_hbm.1, f32[2,256,128]{2,1,0:T(8,128)} %constant.4.clone.table_hbm, ...), custom_call_target="tpu_custom_call" | custom-call | tf_op jit(solution)/shard_map/pallas_call | solution.py:293
  18.4 0.7 %copy.10 = bf16[256,512]{1,0:T(8,128)(2,1)} copy(bf16[256,512]{1,0:T(8,128)(2,1)S(1)} %shard_map.82) | data formatting | bytes 524288
